TPU v7x, 512 devices: a whole 4x4x16 slice. The times are simulated.
512 devices in a mesh: row: 128 (over x, z, y_hi), ch: 4 (over y_lo, core).
Axes of the slice: x: 4, y: 4 (y_hi: 2, y_lo: 2; y = y_hi * 2 + y_lo), z: 16, core: 2. Of those that a mesh axis runs over, the one named last changes fastest.
Arguments:
- pair_rep: bfloat16 [128, 128, 128], P('ch', 'row'), may hold values from -6 to 6
- residue_mask: int32 [128], replicated, may hold values 0 or 1
- chain_ids: int32 [128], replicated, may hold values from 0 to 3, never falling along the last dimension, each value on 1 to 64 neighbouring positions
- in_gain: float32 [2, 128], replicated, may hold values from 0.5 to 1.5
- in_bias: float32 [2, 128], replicated, may hold values from -3 to 3
- w_proj: bfloat16 [2, 128, 4, 128], P(None, None, None, 'ch'), may hold values from -0.5 to 0.5
- w_gate: bfloat16 [2, 128, 128], P(None, None, 'ch'), may hold values from -0.5 to 0.5
- pair_bias: float32 [2, 128], P(None, 'ch'), may hold values from -4 to 4
- out_gain: float32 [2, 128], P(None, 'ch'), may hold values from 0.5 to 1.5
- out_bias: float32 [2, 128], P(None, 'ch'), may hold values from -3 to 3
- w_out: bfloat16 [2, 128, 128], P(None, 'ch'), may hold values from -0.5 to 0.5
Outputs:
- pair_out: bfloat16 [128, 128, 128], P('ch', 'row')
Inputs may be any that keep to these rules, and one draw needn't show every extreme that they name: `chain_ids`: chain numbers never fall along the residues; each chain has 1 to 64 residues.
All inputs are finite; a program needn't handle non-finite values.
Results may differ from a plain program's by a relative error of at most 0.013.
Values may be sent and summed in bfloat16 or wider, within the bound.
No kernel may reach another device: no remote copies, remote signals or barrier semaphores. Data moves between devices by JAX's collectives and lax.ppermute only.
A program may use at most 64 MiB of HBM per device.

v0:
```python
import jax
import jax.numpy as jnp
from jax import lax
from jax.sharding import PartitionSpec as P

epsilon = 1e-05


def in_order(tiles, dim):
    tiles = jnp.moveaxis(tiles, 0, dim)
    dims = tiles.shape
    return tiles.reshape(*dims[:dim], dims[dim] * dims[dim + 1], *dims[dim + 2 :])


def from_everyone(x, axis):
    devices = lax.axis_size(axis)
    return lax.all_to_all(jnp.broadcast_to(x[None], (devices, *x.shape)), axis, 0, 0, tiled=True)


def gathered_copies(x, axis, dim):
    return in_order(from_everyone(x, axis), dim)


def of_everyone(x, axis):
    return from_everyone(x, axis).sum(axis=0)


def together(arrays, axis):
    ends = [0]
    for a in arrays:
        ends.append(ends[-1] + a.size)
    so_far = of_everyone(jnp.concatenate([a.ravel() for a in arrays]), axis)
    return tuple((so_far[b:e].reshape(a.shape) for a, b, e in zip(arrays, ends, ends[1:])))


def in_blocks(x, dim, devices):
    before, after = (x.shape[:dim], x.shape[dim + 1 :])
    return jnp.moveaxis(x.reshape(*before, devices, -1, *after), dim, 0)


def sum_at_owner(x, axis, dim):
    devices = lax.axis_size(axis)
    tiles = lax.all_to_all(in_blocks(x, dim, devices), axis, 0, 0, tiled=True)
    return jnp.sum(tiles.astype(jnp.float32), axis=0)


def sent_together(arrays, axis, split_dim, concat_dim, along):
    widths = [a.shape[along] for a in arrays]
    both = jnp.concatenate(arrays, axis=along)
    result = lax.all_to_all(both, axis, split_axis=split_dim, concat_axis=concat_dim, tiled=True)
    return tuple(jnp.split(result, [sum(widths[:k]) for k in range(1, len(widths))], axis=along))


def channel_norm(values, norm_gain, norm_bias):
    mean_val = jnp.mean(values, axis=0)
    variance = jnp.mean(values * values, axis=0) - mean_val * mean_val
    return (values - mean_val) * lax.rsqrt(variance + epsilon) * norm_gain[
        :, None, None
    ] + norm_bias[:, None, None]


def prepare(
    pair_local, layer, in_gain, in_bias, w_proj, w_gate, pair_bias, mask_rows, mask_cols, same_chain
):
    full_pair = gathered_copies(pair_local, "ch", 0)
    normed = channel_norm(full_pair.astype(jnp.float32), in_gain[layer], in_bias[layer]).astype(
        jnp.bfloat16
    )
    projected = jnp.einsum(
        "cij,cpd->pdij", normed, w_proj[layer], preferred_element_type=jnp.float32
    )
    pair_mask = mask_rows[:, None] * mask_cols[None, :]
    first_arm = (jax.nn.sigmoid(projected[0]) * projected[1] * pair_mask).astype(jnp.bfloat16)
    second_arm = (jax.nn.sigmoid(projected[2]) * projected[3] * pair_mask).astype(jnp.bfloat16)
    logits = jnp.einsum("cij,cd->dij", normed, w_gate[layer], preferred_element_type=jnp.float32)
    logits = logits + pair_bias[layer][:, None, None] * same_chain[None]
    return (first_arm, second_arm, jax.nn.sigmoid(logits))


def finish(product_sum, gating, layer, out_gain, out_bias, w_out):
    totals = together(
        (jnp.sum(product_sum, axis=0), jnp.sum(product_sum * product_sum, axis=0)), "ch"
    )
    channels = product_sum.shape[0] * lax.axis_size("ch")
    mean_val = totals[0] / channels
    variance = totals[1] / channels - mean_val * mean_val
    scaled = (product_sum - mean_val) * lax.rsqrt(variance + epsilon)
    normed = (scaled * out_gain[layer][:, None, None] + out_bias[layer][:, None, None]).astype(
        jnp.bfloat16
    )
    columns = w_out[layer]
    mixed = sum_at_owner(
        jnp.einsum("dij,dc->cij", normed, columns, preferred_element_type=jnp.float32).astype(
            jnp.bfloat16
        ),
        "ch",
        0,
    )
    return gating * mixed


def to_owner(first_arm, second_arm):
    first_quarter, second_quarter = sent_together((first_arm, second_arm), "ch", 2, 0, 1)
    return sent_together((first_quarter, second_quarter), "row", 0, 1, 2)


def to_rows(owned):
    blocks = lax.all_to_all(owned, "row", split_axis=1, concat_axis=0, tiled=True)
    return lax.all_to_all(blocks, "ch", split_axis=0, concat_axis=2, tiled=True)


def body(
    pair_rep,
    residue_mask,
    chain_ids,
    in_gain,
    in_bias,
    w_proj,
    w_gate,
    pair_bias,
    out_gain,
    out_bias,
    w_out,
):
    rows_here = pair_rep.shape[1]
    row_start = lax.axis_index("row") * rows_here
    mask_cols = residue_mask.astype(jnp.float32)
    mask_rows = lax.dynamic_slice_in_dim(mask_cols, row_start, rows_here)
    chain_rows = lax.dynamic_slice_in_dim(chain_ids, row_start, rows_here)
    same_chain = (chain_rows[:, None] == chain_ids[None, :]).astype(jnp.float32)
    first_arm, second_arm, gating = prepare(
        pair_rep, 0, in_gain, in_bias, w_proj, w_gate, pair_bias, mask_rows, mask_cols, same_chain
    )
    first_own, second_own = to_owner(first_arm, second_arm)
    partial_sum = jnp.einsum(
        "dik,djk->dij", first_own, second_own, preferred_element_type=jnp.float32
    )
    owned_sum = sum_at_owner(partial_sum.astype(jnp.bfloat16), "ch", 2)
    product_sum = to_rows(owned_sum)
    middle = (
        pair_rep.astype(jnp.float32) + finish(product_sum, gating, 0, out_gain, out_bias, w_out)
    ).astype(jnp.bfloat16)
    in_first, in_second, in_gating = prepare(
        middle, 1, in_gain, in_bias, w_proj, w_gate, pair_bias, mask_rows, mask_cols, same_chain
    )
    left_own, right_own = to_owner(in_first, in_second)
    owned_product = jnp.einsum(
        "dki,dkj->dij",
        gathered_copies(left_own, "ch", 2),
        right_own,
        preferred_element_type=jnp.float32,
    )
    in_product = to_rows(owned_product)
    update = finish(in_product, in_gating, 1, out_gain, out_bias, w_out)
    return (middle.astype(jnp.float32) + update).astype(jnp.bfloat16)


def solution(mesh):
    return jax.shard_map(
        body,
        mesh=mesh,
        in_specs=(
            P("ch", "row", None),
            P(),
            P(),
            P(),
            P(),
            P(None, None, None, "ch"),
            P(None, None, "ch"),
            P(None, "ch"),
            P(None, "ch"),
            P(None, "ch"),
            P(None, "ch", None),
        ),
        out_specs=P("ch", "row", None),
        check_vma=False,
    )
```

profile of v0, /device:TPU:1, one launch (start us, length us, event | category | flops | bytes accessed | tf_op | source)
XLA Modules:
  0.0 200.2 jit_solution(12180103836867893405)
XLA Ops:
  0.0 1.3 broadcast_in_dim.17
  1.3 10.1 %all-to-all-start = ((bf16[4,32,1,128]{3,1,2,0:T(8,128)(2,1)}), bf16[4,32,1,128]{3,1,2,0:T(8,128)(2,1)S(1)}, u32[]{:S(2)}, u32[]{:S(2)}) async-start(bf16[4,32,1,128]{3,1,2,0:T(8,128)(2,1)} %broadcast_in_dim.17), calls=%async_computation | async-start | bytes 65536 | tf_op jit(solution)/shard_map/all_to_all | solution.py:17
  15.2 6.2 %all_to_all.162 = bf16[4,2,1024]{2,1,0:T(2,128)(2,1)S(1)} all-to-all(bf16[4,2,1024]{2,1,0:T(2,128)(2,1)S(1)} %reshape.1148), channel_id=1, replica_groups=mesh['row'=128,'ch'=4] {'ch'}, dimensions={0} | all-to-all | bytes 32768 | tf_op jit(solution)/shard_map/all_to_all | solution.py:50
  21.9 32.3 %all_to_all.163 = bf16[128,1,64]{2,1,0:T(2,128)(2,1)S(1)} all-to-all(bf16[128,1,64]{2,1,0:T(2,128)(2,1)S(1)} %copy.83), channel_id=1, replica_groups=mesh['row'=128,'ch'=4] {'row'}, dimensions={0} | all-to-all | bytes 32768 | tf_op jit(solution)/shard_map/all_to_all | solution.py:50
  54.5 7.7 %all_to_all.164 = bf16[4,1,128,32]{2,3,1,0:T(8,128)(2,1)S(1)} all-to-all(bf16[4,1,128,32]{2,3,1,0:T(8,128)(2,1)S(1)} %bitcast.246), channel_id=1, replica_groups=mesh['row'=128,'ch'=4] {'ch'}, dimensions={0} | all-to-all | bytes 65536 | tf_op jit(solution)/shard_map/all_to_all | solution.py:43
  62.3 21.3 %all_to_all.165 = f32[1,128,32]{2,0,1:T(1,128)S(1)} all-to-all(f32[1,128,32]{2,0,1:T(1,128)S(1)} %copy.86), channel_id=1, replica_groups=mesh['row'=128,'ch'=4] {'row'}, dimensions={1} | all-to-all | bytes 32768 | tf_op jit(solution)/shard_map/all_to_all | solution.py:108
  85.6 5.5 %all-to-all-start.5 = ((f32[4,1,1024]{2,1,0:T(1,128)}), f32[4,1,1024]{2,1,0:T(1,128)S(1)}, u32[]{:S(2)}, u32[]{:S(2)}) async-start(f32[4,1,1024]{2,1,0:T(1,128)} %reshape.1150), calls=%async_computation.5 | async-start | bytes 32768 | tf_op jit(solution)/shard_map/all_to_all | solution.py:109
  91.1 3.1 %all-to-all-done.5 = f32[4,1,1024]{2,1,0:T(1,128)S(1)} async-done(((f32[4,1,1024]{2,1,0:T(1,128)}), f32[4,1,1024]{2,1,0:T(1,128)S(1)}, u32[]{:S(2)}, u32[]{:S(2)}) %all-to-all-start.5) | async-done | bytes 16416 | tf_op jit(solution)/shard_map/all_to_all | solution.py:109
  96.2 4.1 %all-to-all-start.6 = ((f32[4,1,256]{2,1,0:T(1,128)}), f32[4,1,256]{2,1,0:T(1,128)S(1)}, u32[]{:S(2)}, u32[]{:S(2)}) async-start(f32[4,1,256]{2,1,0:T(1,128)} %broadcast_in_dim.18), calls=%async_computation.6 | async-start | bytes 8192 | tf_op jit(solution)/shard_map/all_to_all | solution.py:17
  101.8 1.6 all-to-all-done.6
  103.4 0.8 convolution_convert_fusion.1
  104.3 3.9 %all-to-all-start.7 = ((bf16[4,32,1,128]{3,1,2,0:T(8,128)(2,1)}), bf16[4,32,1,128]{3,1,2,0:T(8,128)(2,1)S(1)}, u32[]{:S(2)}, u32[]{:S(2)}) async-start(bf16[4,32,1,128]{3,1,2,0:T(8,128)(2,1)} %bitcast.36), calls=%async_computation.7 | async-start | bytes 65536 | tf_op jit(solution)/shard_map/all_to_all | solution.py:43
  108.9 2.5 %all-to-all-done.7 = bf16[4,32,1,128]{3,1,2,0:T(8,128)(2,1)S(1)} async-done(((bf16[4,32,1,128]{3,1,2,0:T(8,128)(2,1)}), bf16[4,32,1,128]{3,1,2,0:T(8,128)(2,1)S(1)}, u32[]{:S(2)}, u32[]{:S(2)}) %all-to-all-start.7) | async-done | bytes 32800 | tf_op jit(solution)/shard_map/all_to_all | solution.py:43
  111.7 6.3 %all_to_all.166 = bf16[4,32,1,128]{3,1,2,0:T(8,128)(2,1)S(1)} all-to-all(bf16[4,32,1,128]{3,1,2,0:T(8,128)(2,1)S(1)} %broadcast_in_dim.20), channel_id=1, replica_groups=mesh['row'=128,'ch'=4] {'ch'}, dimensions={0} | all-to-all | bytes 65536 | tf_op jit(solution)/shard_map/all_to_all | solution.py:17
  118.5 6.2 %all_to_all.167 = bf16[4,2,1024]{2,1,0:T(2,128)(2,1)S(1)} all-to-all(bf16[4,2,1024]{2,1,0:T(2,128)(2,1)S(1)} %reshape.1152), channel_id=1, replica_groups=mesh['row'=128,'ch'=4] {'ch'}, dimensions={0} | all-to-all | bytes 32768 | tf_op jit(solution)/shard_map/all_to_all | solution.py:50
  125.2 21.3 %all_to_all.168 = bf16[128,1,64]{2,1,0:T(2,128)(2,1)S(1)} all-to-all(bf16[128,1,64]{2,1,0:T(2,128)(2,1)S(1)} %copy.96), channel_id=1, replica_groups=mesh['row'=128,'ch'=4] {'row'}, dimensions={0} | all-to-all | bytes 32768 | tf_op jit(solution)/shard_map/all_to_all | solution.py:50
  146.6 7.6 %all_to_all.169 = bf16[4,1,128,32]{2,3,1,0:T(8,128)(2,1)S(1)} all-to-all(bf16[4,1,128,32]{2,3,1,0:T(8,128)(2,1)S(1)} %broadcast_in_dim.22), channel_id=1, replica_groups=mesh['row'=128,'ch'=4] {'ch'}, dimensions={0} | all-to-all | bytes 65536 | tf_op jit(solution)/shard_map/all_to_all | solution.py:17
  154.4 21.3 %all_to_all.170 = f32[1,128,32]{2,0,1:T(1,128)S(1)} all-to-all(f32[1,128,32]{2,0,1:T(1,128)S(1)} %bitcast.238), channel_id=1, replica_groups=mesh['row'=128,'ch'=4] {'row'}, dimensions={1} | all-to-all | bytes 32768 | tf_op jit(solution)/shard_map/all_to_all | solution.py:108
  175.6 0.8 reduce.23
  176.5 7.6 %all_to_all.171 = f32[4,1,1024]{2,1,0:T(1,128)S(1)} all-to-all(f32[4,1,1024]{2,1,0:T(1,128)S(1)} %reshape.1154), channel_id=1, replica_groups=mesh['row'=128,'ch'=4] {'ch'}, dimensions={0} | all-to-all | bytes 32768 | tf_op jit(solution)/shard_map/all_to_all | solution.py:109
  185.8 3.9 %all-to-all-start.14 = ((f32[4,1,256]{2,1,0:T(1,128)}), f32[4,1,256]{2,1,0:T(1,128)S(1)}, u32[]{:S(2)}, u32[]{:S(2)}) async-start(f32[4,1,256]{2,1,0:T(1,128)} %broadcast_in_dim.23), calls=%async_computation.14 | async-start | bytes 8192 | tf_op jit(solution)/shard_map/all_to_all | solution.py:17
  189.9 3.0 %all-to-all-done.14 = f32[4,1,256]{2,1,0:T(1,128)S(1)} async-done(((f32[4,1,256]{2,1,0:T(1,128)}), f32[4,1,256]{2,1,0:T(1,128)S(1)}, u32[]{:S(2)}, u32[]{:S(2)}) %all-to-all-start.14) | async-done | bytes 4128 | tf_op jit(solution)/shard_map/all_to_all | solution.py:17
  193.1 6.2 %all_to_all.172 = bf16[4,32,1,128]{3,1,2,0:T(8,128)(2,1)S(1)} all-to-all(bf16[4,32,1,128]{3,1,2,0:T(8,128)(2,1)S(1)} %bitcast.245), channel_id=1, replica_groups=mesh['row'=128,'ch'=4] {'ch'}, dimensions={0} | all-to-all | bytes 65536 | tf_op jit(solution)/shard_map/all_to_all | solution.py:43
  199.4 0.8 fusion.16
  (100 shorter events, 14.2 us)
Async XLA Ops:
  0.0 11.4 %copy-start = (bf16[2,128,4,32]{1,3,2,0:T(8,128)(2,1)S(1)}, bf16[2,128,4,32]{1,3,2,0:T(8,128)(2,1)}, u32[]{:S(2)}) copy-start(bf16[2,128,4,32]{1,3,2,0:T(8,128)(2,1)} %param.16) | copy-start | bytes 196612
  1.3 13.3 %all-to-all-start = ((bf16[4,32,1,128]{3,1,2,0:T(8,128)(2,1)}), bf16[4,32,1,128]{3,1,2,0:T(8,128)(2,1)S(1)}, u32[]{:S(2)}, u32[]{:S(2)}) async-start(bf16[4,32,1,128]{3,1,2,0:T(8,128)(2,1)} %broadcast_in_dim.17), calls=%async_computation | async-start | bytes 65536 | tf_op jit(solution)/shard_map/all_to_all | solution.py:17
  11.5 0.7 copy-start.4
  11.5 0.7 copy-start.9
  12.1 0.7 copy-start.3
  85.6 5.5 %copy-start.5 = (f32[2,32]{1,0:T(2,128)S(1)}, f32[2,32]{1,0:T(2,128)}, u32[]{:S(2)}) copy-start(f32[2,32]{1,0:T(2,128)} %param.20) | copy-start | bytes 772
  85.6 5.5 %copy-start.6 = (f32[2,32]{1,0:T(2,128)S(1)}, f32[2,32]{1,0:T(2,128)}, u32[]{:S(2)}) copy-start(f32[2,32]{1,0:T(2,128)} %param.19) | copy-start | bytes 772
  85.6 8.6 %all-to-all-start.5 = ((f32[4,1,1024]{2,1,0:T(1,128)}), f32[4,1,1024]{2,1,0:T(1,128)S(1)}, u32[]{:S(2)}, u32[]{:S(2)}) async-start(f32[4,1,1024]{2,1,0:T(1,128)} %reshape.1150), calls=%async_computation.5 | async-start | bytes 32768 | tf_op jit(solution)/shard_map/all_to_all | solution.py:109
  96.2 4.1 %copy-start.2 = (f32[2,32]{1,0:T(2,128)S(1)}, f32[2,32]{1,0:T(2,128)}, u32[]{:S(2)}) copy-start(f32[2,32]{1,0:T(2,128)} %param.18) | copy-start | bytes 772
  96.2 7.2 %all-to-all-start.6 = ((f32[4,1,256]{2,1,0:T(1,128)}), f32[4,1,256]{2,1,0:T(1,128)S(1)}, u32[]{:S(2)}, u32[]{:S(2)}) async-start(f32[4,1,256]{2,1,0:T(1,128)} %broadcast_in_dim.18), calls=%async_computation.6 | async-start | bytes 8192 | tf_op jit(solution)/shard_map/all_to_all | solution.py:17
  100.3 0.7 copy-start.10
  101.7 1.7 copy-start.7
  104.3 7.1 %all-to-all-start.7 = ((bf16[4,32,1,128]{3,1,2,0:T(8,128)(2,1)}), bf16[4,32,1,128]{3,1,2,0:T(8,128)(2,1)S(1)}, u32[]{:S(2)}, u32[]{:S(2)}) async-start(bf16[4,32,1,128]{3,1,2,0:T(8,128)(2,1)} %bitcast.36), calls=%async_computation.7 | async-start | bytes 65536 | tf_op jit(solution)/shard_map/all_to_all | solution.py:43
  108.9 2.5 %copy-start.1 = (bf16[32,1,128]{2,0,1:T(8,128)(2,1)S(1)}, bf16[32,1,128]{2,0,1:T(8,128)(2,1)}, u32[]{:S(2)}) copy-start(bf16[32,1,128]{2,0,1:T(8,128)(2,1)} %param.11) | copy-start | bytes 24580
  108.9 2.5 %copy-start.8 = (bf16[2,128,32]{1,2,0:T(8,128)(2,1)S(1)}, bf16[2,128,32]{1,2,0:T(8,128)(2,1)}, u32[]{:S(2)}) copy-start(bf16[2,128,32]{1,2,0:T(8,128)(2,1)} %param.17) | copy-start | bytes 49156
  185.8 7.0 %all-to-all-start.14 = ((f32[4,1,256]{2,1,0:T(1,128)}), f32[4,1,256]{2,1,0:T(1,128)S(1)}, u32[]{:S(2)}, u32[]{:S(2)}) async-start(f32[4,1,256]{2,1,0:T(1,128)} %broadcast_in_dim.23), calls=%async_computation.14 | async-start | bytes 8192 | tf_op jit(solution)/shard_map/all_to_all | solution.py:17
where the time goes:
time: 201 us; the launch traced here: 200 us
  blocking collectives  144 us (72%)
  starting transfers between devices  27.5 us (14%)
  waiting for transfers between devices  10.7 us (5%)
  local copies, waits for them, and re-layouts  9.85 us (5%)
  other arithmetic  4.72 us (2%)
  matrix products  2.92 us (1%)
    all_to_all x4, blocking collectives, sent_together(): lax.all_to_all(both, axis, split_axis=split_dim, concat_axis=concat_dim,...  66.1 us
    all_to_all x2, blocking collectives, to_rows(): lax.all_to_all(owned, 'row', split_axis=1, concat_axis=0, tiled=True)  42.5 us
    all_to_all x3, starting transfers between devices, from_everyone(): lax.all_to_all(jnp.broadcast_to(x[None], (devices, *x.shape)), axis, 0, 0...  18.1 us
    all_to_all x2, blocking collectives, from_everyone(): lax.all_to_all(jnp.broadcast_to(x[None], (devices, *x.shape)), axis, 0, 0...  13.9 us
    all_to_all x2, blocking collectives, sum_at_owner(): tiles = lax.all_to_all(in_blocks(x, dim, devices), axis, 0, 0, tiled=True)  13.9 us
    all_to_all x1, blocking collectives, to_rows(): return lax.all_to_all(blocks, 'ch', split_axis=0, concat_axis=2, tiled=True)  7.58 us
    all_to_all x1, starting transfers between devices, to_rows(): return lax.all_to_all(blocks, 'ch', split_axis=0, concat_axis=2, tiled=True)  5.46 us
    all_to_all x3, waiting for transfers between devices, from_everyone(): lax.all_to_all(jnp.broadcast_to(x[None], (devices, *x.shape)), axis, 0, 0...  5.1 us
  transfers between devices with their start and end apart: 5, of which 5 were waited for; matrix products, arithmetic and copies ran while one was open for 1% of the time, Pallas kernels for 0%

commit v1 on v0

--- a/solution.py
+++ b/solution.py
@@ -105,7 +105,10 @@
 
 
 def to_rows(owned):
-    blocks = lax.all_to_all(owned, "row", split_axis=1, concat_axis=0, tiled=True)
+    blocks = jnp.concatenate(
+        lax.all_to_all(jnp.stack(jnp.split(owned, lax.axis_size("row"), axis=1)), "row", 0, 0),
+        axis=0,
+    )
     return lax.all_to_all(blocks, "ch", split_axis=0, concat_axis=2, tiled=True)
 
 

time: 201 us -> 212 us (1.055)
  local copies, waits for them, and re-layouts: 9.85 us -> 19.3 us
    split x0 -> x14, local copies, waits for them, and re-layouts: none -> 7.6 us  [to_rows(): jnp.split(owned, lax.axis_size('row'), axis=1)]
    unnamed x30 -> x284, local copies, waits for them, and re-layouts: 3.54 us -> 5.81 us
where the time goes in v1:
time: 212 us; the launch traced here: 211 us
  blocking collectives  144 us (68%)
  starting transfers between devices  27.5 us (13%)
  local copies, waits for them, and re-layouts  19.3 us (9%)
  waiting for transfers between devices  10.8 us (5%)
  other arithmetic  4.65 us (2%)
  matrix products  2.92 us (1%)
    all_to_all x4, blocking collectives, sent_together(): lax.all_to_all(both, axis, split_axis=split_dim, concat_axis=concat_dim,...  66.3 us
    all_to_all x2, blocking collectives, to_rows(): lax.all_to_all(jnp.stack(jnp.split(owned, lax.axis_size('row'), axis=1)),...  42.5 us
    all_to_all x3, starting transfers between devices, from_everyone(): lax.all_to_all(jnp.broadcast_to(x[None], (devices, *x.shape)), axis, 0, 0...  18.1 us
    all_to_all x2, blocking collectives, from_everyone(): lax.all_to_all(jnp.broadcast_to(x[None], (devices, *x.shape)), axis, 0, 0...  13.9 us
    all_to_all x2, blocking collectives, sum_at_owner(): tiles = lax.all_to_all(in_blocks(x, dim, devices), axis, 0, 0, tiled=True)  13.9 us
    split x14, local copies, waits for them, and re-layouts, to_rows(): jnp.split(owned, lax.axis_size('row'), axis=1)  7.6 us
    all_to_all x1, blocking collectives, to_rows(): return lax.all_to_all(blocks, 'ch', split_axis=0, concat_axis=2, tiled=True)  7.58 us
    unnamed x284, local copies, waits for them, and re-layouts  5.81 us
  transfers between devices with their start and end apart: 5, of which 5 were waited for; matrix products, arithmetic and copies ran while one was open for 1% of the time, Pallas kernels for 0%

profile of v1, /device:TPU:1, one launch (start us, length us, event | category | flops | bytes accessed | tf_op | source)
XLA Modules:
  0.0 210.7 jit_solution(2166150122327003415)
XLA Ops:
  0.0 1.3 broadcast_in_dim.17
  1.3 10.1 %all-to-all-start = ((bf16[4,32,1,128]{3,1,2,0:T(8,128)(2,1)}), bf16[4,32,1,128]{3,1,2,0:T(8,128)(2,1)S(1)}, u32[]{:S(2)}, u32[]{:S(2)}) async-start(bf16[4,32,1,128]{3,1,2,0:T(8,128)(2,1)} %broadcast_in_dim.17), calls=%async_computation | async-start | bytes 65536 | tf_op jit(solution)/shard_map/all_to_all | solution.py:17
  15.2 6.2 %all_to_all.148 = bf16[4,2,1024]{2,1,0:T(2,128)(2,1)S(1)} all-to-all(bf16[4,2,1024]{2,1,0:T(2,128)(2,1)S(1)} %reshape.1406), channel_id=1, replica_groups=mesh['row'=128,'ch'=4] {'ch'}, dimensions={0} | all-to-all | bytes 32768 | tf_op jit(solution)/shard_map/all_to_all | solution.py:50
  21.9 32.3 %all_to_all.149 = bf16[128,1,64]{2,1,0:T(2,128)(2,1)S(1)} all-to-all(bf16[128,1,64]{2,1,0:T(2,128)(2,1)S(1)} %copy.856), channel_id=1, replica_groups=mesh['row'=128,'ch'=4] {'row'}, dimensions={0} | all-to-all | bytes 32768 | tf_op jit(solution)/shard_map/all_to_all | solution.py:50
  54.5 7.7 %all_to_all.150 = bf16[4,1,128,32]{2,3,1,0:T(8,128)(2,1)S(1)} all-to-all(bf16[4,1,128,32]{2,3,1,0:T(8,128)(2,1)S(1)} %bitcast.771), channel_id=1, replica_groups=mesh['row'=128,'ch'=4] {'ch'}, dimensions={0} | all-to-all | bytes 65536 | tf_op jit(solution)/shard_map/all_to_all | solution.py:43
  67.5 21.3 %all_to_all.151 = f32[128,1,1,32]{3,2,1,0:T(1,128)S(1)} all-to-all(f32[128,1,1,32]{3,2,1,0:T(1,128)S(1)} %constant_dynamic-update-slice_fusion), channel_id=1, replica_groups=mesh['row'=128,'ch'=4] {'row'}, dimensions={0} | all-to-all | bytes 32768 | tf_op jit(solution)/shard_map/all_to_all | solution.py:109
  90.8 5.5 %all-to-all-start.5 = ((f32[4,1,1024]{2,1,0:T(1,128)}), f32[4,1,1024]{2,1,0:T(1,128)S(1)}, u32[]{:S(2)}, u32[]{:S(2)}) async-start(f32[4,1,1024]{2,1,0:T(1,128)} %reshape.1408), calls=%async_computation.5 | async-start | bytes 32768 | tf_op jit(solution)/shard_map/all_to_all | solution.py:112
  96.3 3.1 %all-to-all-done.5 = f32[4,1,1024]{2,1,0:T(1,128)S(1)} async-done(((f32[4,1,1024]{2,1,0:T(1,128)}), f32[4,1,1024]{2,1,0:T(1,128)S(1)}, u32[]{:S(2)}, u32[]{:S(2)}) %all-to-all-start.5) | async-done | bytes 16416 | tf_op jit(solution)/shard_map/all_to_all | solution.py:112
  101.1 4.1 %all-to-all-start.6 = ((f32[4,1,256]{2,1,0:T(1,128)}), f32[4,1,256]{2,1,0:T(1,128)S(1)}, u32[]{:S(2)}, u32[]{:S(2)}) async-start(f32[4,1,256]{2,1,0:T(1,128)} %broadcast_in_dim.18), calls=%async_computation.6 | async-start | bytes 8192 | tf_op jit(solution)/shard_map/all_to_all | solution.py:17
  106.7 1.6 all-to-all-done.6
  108.3 0.8 convolution_convert_fusion.1
  109.2 3.9 %all-to-all-start.7 = ((bf16[4,32,1,128]{3,1,2,0:T(8,128)(2,1)}), bf16[4,32,1,128]{3,1,2,0:T(8,128)(2,1)S(1)}, u32[]{:S(2)}, u32[]{:S(2)}) async-start(bf16[4,32,1,128]{3,1,2,0:T(8,128)(2,1)} %bitcast.37), calls=%async_computation.7 | async-start | bytes 65536 | tf_op jit(solution)/shard_map/all_to_all | solution.py:43
  113.8 2.5 %all-to-all-done.7 = bf16[4,32,1,128]{3,1,2,0:T(8,128)(2,1)S(1)} async-done(((bf16[4,32,1,128]{3,1,2,0:T(8,128)(2,1)}), bf16[4,32,1,128]{3,1,2,0:T(8,128)(2,1)S(1)}, u32[]{:S(2)}, u32[]{:S(2)}) %all-to-all-start.7) | async-done | bytes 32800 | tf_op jit(solution)/shard_map/all_to_all | solution.py:43
  116.6 6.3 %all_to_all.152 = bf16[4,32,1,128]{3,1,2,0:T(8,128)(2,1)S(1)} all-to-all(bf16[4,32,1,128]{3,1,2,0:T(8,128)(2,1)S(1)} %broadcast_in_dim.20), channel_id=1, replica_groups=mesh['row'=128,'ch'=4] {'ch'}, dimensions={0} | all-to-all | bytes 65536 | tf_op jit(solution)/shard_map/all_to_all | solution.py:17
  123.4 6.2 %all_to_all.153 = bf16[4,2,1024]{2,1,0:T(2,128)(2,1)S(1)} all-to-all(bf16[4,2,1024]{2,1,0:T(2,128)(2,1)S(1)} %reshape.1410), channel_id=1, replica_groups=mesh['row'=128,'ch'=4] {'ch'}, dimensions={0} | all-to-all | bytes 32768 | tf_op jit(solution)/shard_map/all_to_all | solution.py:50
  130.1 21.5 %all_to_all.154 = bf16[128,1,64]{2,1,0:T(2,128)(2,1)S(1)} all-to-all(bf16[128,1,64]{2,1,0:T(2,128)(2,1)S(1)} %copy.866), channel_id=1, replica_groups=mesh['row'=128,'ch'=4] {'row'}, dimensions={0} | all-to-all | bytes 32768 | tf_op jit(solution)/shard_map/all_to_all | solution.py:50
  151.7 7.6 %all_to_all.155 = bf16[4,1,128,32]{2,3,1,0:T(8,128)(2,1)S(1)} all-to-all(bf16[4,1,128,32]{2,3,1,0:T(8,128)(2,1)S(1)} %broadcast_in_dim.22), channel_id=1, replica_groups=mesh['row'=128,'ch'=4] {'ch'}, dimensions={0} | all-to-all | bytes 65536 | tf_op jit(solution)/shard_map/all_to_all | solution.py:17
  164.8 21.3 %all_to_all.156 = f32[128,1,1,32]{3,2,1,0:T(1,128)S(1)} all-to-all(f32[128,1,1,32]{3,2,1,0:T(1,128)S(1)} %constant_dynamic-update-slice_fusion.128), channel_id=1, replica_groups=mesh['row'=128,'ch'=4] {'row'}, dimensions={0} | all-to-all | bytes 32768 | tf_op jit(solution)/shard_map/all_to_all | solution.py:109
  186.1 0.8 reduce.535
  187.0 7.6 %all_to_all.157 = f32[4,1,1024]{2,1,0:T(1,128)S(1)} all-to-all(f32[4,1,1024]{2,1,0:T(1,128)S(1)} %reshape.1412), channel_id=1, replica_groups=mesh['row'=128,'ch'=4] {'ch'}, dimensions={0} | all-to-all | bytes 32768 | tf_op jit(solution)/shard_map/all_to_all | solution.py:112
  196.3 3.9 %all-to-all-start.14 = ((f32[4,1,256]{2,1,0:T(1,128)}), f32[4,1,256]{2,1,0:T(1,128)S(1)}, u32[]{:S(2)}, u32[]{:S(2)}) async-start(f32[4,1,256]{2,1,0:T(1,128)} %broadcast_in_dim.23), calls=%async_computation.14 | async-start | bytes 8192 | tf_op jit(solution)/shard_map/all_to_all | solution.py:17
  200.4 3.0 %all-to-all-done.14 = f32[4,1,256]{2,1,0:T(1,128)S(1)} async-done(((f32[4,1,256]{2,1,0:T(1,128)}), f32[4,1,256]{2,1,0:T(1,128)S(1)}, u32[]{:S(2)}, u32[]{:S(2)}) %all-to-all-start.14) | async-done | bytes 4128 | tf_op jit(solution)/shard_map/all_to_all | solution.py:17
  203.6 6.2 %all_to_all.158 = bf16[4,32,1,128]{3,1,2,0:T(8,128)(2,1)S(1)} all-to-all(bf16[4,32,1,128]{3,1,2,0:T(8,128)(2,1)S(1)} %bitcast.770), channel_id=1, replica_groups=mesh['row'=128,'ch'=4] {'ch'}, dimensions={0} | all-to-all | bytes 65536 | tf_op jit(solution)/shard_map/all_to_all | solution.py:43
  209.8 0.8 fusion.16
  (366 shorter events, 23.7 us)
Async XLA Ops:
  0.0 11.4 %copy-start = (bf16[2,128,4,32]{1,3,2,0:T(8,128)(2,1)S(1)}, bf16[2,128,4,32]{1,3,2,0:T(8,128)(2,1)}, u32[]{:S(2)}) copy-start(bf16[2,128,4,32]{1,3,2,0:T(8,128)(2,1)} %param.16) | copy-start | bytes 196612
  1.3 13.3 %all-to-all-start = ((bf16[4,32,1,128]{3,1,2,0:T(8,128)(2,1)}), bf16[4,32,1,128]{3,1,2,0:T(8,128)(2,1)S(1)}, u32[]{:S(2)}, u32[]{:S(2)}) async-start(bf16[4,32,1,128]{3,1,2,0:T(8,128)(2,1)} %broadcast_in_dim.17), calls=%async_computation | async-start | bytes 65536 | tf_op jit(solution)/shard_map/all_to_all | solution.py:17
  11.4 0.7 copy-start.9
  12.1 0.7 copy-start.4
  12.1 0.7 copy-start.3
  90.8 5.5 %copy-start.5 = (f32[2,32]{1,0:T(2,128)S(1)}, f32[2,32]{1,0:T(2,128)}, u32[]{:S(2)}) copy-start(f32[2,32]{1,0:T(2,128)} %param.20) | copy-start | bytes 772
  90.8 5.5 %copy-start.6 = (f32[2,32]{1,0:T(2,128)S(1)}, f32[2,32]{1,0:T(2,128)}, u32[]{:S(2)}) copy-start(f32[2,32]{1,0:T(2,128)} %param.19) | copy-start | bytes 772
  90.8 8.6 %all-to-all-start.5 = ((f32[4,1,1024]{2,1,0:T(1,128)}), f32[4,1,1024]{2,1,0:T(1,128)S(1)}, u32[]{:S(2)}, u32[]{:S(2)}) async-start(f32[4,1,1024]{2,1,0:T(1,128)} %reshape.1408), calls=%async_computation.5 | async-start | bytes 32768 | tf_op jit(solution)/shard_map/all_to_all | solution.py:112
  101.1 4.1 %copy-start.2 = (f32[2,32]{1,0:T(2,128)S(1)}, f32[2,32]{1,0:T(2,128)}, u32[]{:S(2)}) copy-start(f32[2,32]{1,0:T(2,128)} %param.18) | copy-start | bytes 772
  101.1 7.2 %all-to-all-start.6 = ((f32[4,1,256]{2,1,0:T(1,128)}), f32[4,1,256]{2,1,0:T(1,128)S(1)}, u32[]{:S(2)}, u32[]{:S(2)}) async-start(f32[4,1,256]{2,1,0:T(1,128)} %broadcast_in_dim.18), calls=%async_computation.6 | async-start | bytes 8192 | tf_op jit(solution)/shard_map/all_to_all | solution.py:17
  105.2 0.7 copy-start.10
  106.6 1.8 copy-start.7
  109.2 7.1 %all-to-all-start.7 = ((bf16[4,32,1,128]{3,1,2,0:T(8,128)(2,1)}), bf16[4,32,1,128]{3,1,2,0:T(8,128)(2,1)S(1)}, u32[]{:S(2)}, u32[]{:S(2)}) async-start(bf16[4,32,1,128]{3,1,2,0:T(8,128)(2,1)} %bitcast.37), calls=%async_computation.7 | async-start | bytes 65536 | tf_op jit(solution)/shard_map/all_to_all | solution.py:43
  113.8 2.5 %copy-start.1 = (bf16[32,1,128]{2,0,1:T(8,128)(2,1)S(1)}, bf16[32,1,128]{2,0,1:T(8,128)(2,1)}, u32[]{:S(2)}) copy-start(bf16[32,1,128]{2,0,1:T(8,128)(2,1)} %param.11) | copy-start | bytes 24580
  113.8 2.5 %copy-start.8 = (bf16[2,128,32]{1,2,0:T(8,128)(2,1)S(1)}, bf16[2,128,32]{1,2,0:T(8,128)(2,1)}, u32[]{:S(2)}) copy-start(bf16[2,128,32]{1,2,0:T(8,128)(2,1)} %param.17) | copy-start | bytes 49156
  196.3 7.0 %all-to-all-start.14 = ((f32[4,1,256]{2,1,0:T(1,128)}), f32[4,1,256]{2,1,0:T(1,128)S(1)}, u32[]{:S(2)}, u32[]{:S(2)}) async-start(f32[4,1,256]{2,1,0:T(1,128)} %broadcast_in_dim.23), calls=%async_computation.14 | async-start | bytes 8192 | tf_op jit(solution)/shard_map/all_to_all | solution.py:17
